TPU v7x, 32 devices: a whole 2x2x4 slice. The times are simulated.
32 devices in a mesh: sk: 8 (over y, x, core), lang: 4 (over z).
Axes of the slice: x: 2, y: 2, z: 4, core: 2. Of those that a mesh axis runs over, the one named last changes fastest.
Arguments:
- embeddings: bfloat16 [32768, 1024], P(('sk', 'lang')), may hold values from -40 to 40
- omega: bfloat16 [32768, 256], P(('sk', 'lang')), may hold values from -0.03125 to 0.03125
- lang_ids: int32 [32768, 1], P(('sk', 'lang')), may hold values from 0 to 11; in each aligned block of 1024 rows (0 to 1023, 1024 to 2047, ...) at most 128 rows name the same one
Outputs:
- grouped: bfloat16 [49152, 256], P(('sk', 'lang'))
Inputs may be any that keep to these rules, and one draw needn't show every extreme that they name: `lang_ids`: among the 1024 sentences of one device no language appears more than 128 times, and some language appears exactly 128 times.
All inputs are finite; a program needn't handle non-finite values.
Results may differ from a plain program's by a relative error of at most 0.0075.
Values may be sent and summed in bfloat16 or wider, within the bound.
A program may use at most 64 MiB of HBM per device.

v0:
```python
import functools

import jax
import jax.numpy as jnp
from jax import lax
from jax.experimental import pallas as pl
from jax.experimental.pallas import tpu as pltpu
from jax.sharding import PartitionSpec as P

SKETCH = 256
LANGS = 12
CAP = 128
HALF = 128
LANE = 128
F32 = jnp.float32
BF16 = jnp.bfloat16
VMEM = pl.BlockSpec(memory_space=pltpu.VMEM)


def fdot(a, b, ca, cb):
    return lax.dot_general(
        a, b, (((ca,), (cb,)), ((), ())),
        precision=lax.Precision.HIGHEST, preferred_element_type=F32,
    )


def bdot(a, b, ca, cb):
    return lax.dot_general(a, b, (((ca,), (cb,)), ((), ())), preferred_element_type=F32)


def lower_inverse(a):
    lane = lax.broadcasted_iota(jnp.int32, (1, LANE), 1)
    sub = lax.broadcasted_iota(jnp.int32, (8, LANE), 0)
    lane8 = lax.broadcasted_iota(jnp.int32, (8, LANE), 1)
    tiles = [a[8 * i : 8 * i + 8, :] for i in range(HALF // 8)]
    result = []
    for k in range(0, HALF, 4):
        t, s = k // 8, k % 8
        cols = {
            i: [jnp.broadcast_to(tiles[i][:, k + j : k + j + 1], (8, LANE)) for j in range(4)]
            for i in range(t, HALF // 8)
        }
        p = [[cols[t][j][s + i : s + i + 1, :] for j in range(i + 1)] for i in range(4)]
        group = (lane >= k) & (lane < k + 4)
        u, m, inv, root = [], [], [], []
        for i in range(4):
            row = tiles[t][s + i : s + i + 1, :]
            u.append(jnp.where(group, (lane == k + i).astype(F32), row))
        for j in range(4):
            inv.append(1.0 / p[j][j])
            root.append(lax.rsqrt(p[j][j]))
            m.append({i: p[i][j] * inv[j] for i in range(j + 1, 4)})
            for i in range(j + 1, 4):
                for c in range(j + 1, i + 1):
                    p[i][c] = p[i][c] - m[j][i] * p[c][j]
                u[i] = u[i] - m[j][i] * u[j]
        v = [None] * 4
        for j in (3, 2, 1, 0):
            v[j] = u[j] * inv[j]
            for i in range(j + 1, 4):
                v[j] = v[j] - m[j][i] * v[i]
        rows = jnp.zeros((8, LANE), F32)
        for j in range(4):
            rows = jnp.where(sub == s + j, u[j] * root[j], rows)
        rows = jnp.where(lane8 <= sub + 8 * t, rows, 0.0)
        if s == 0:
            result.append(rows)
        else:
            result[t] = result[t] + rows
        for i in range(t if s == 0 else t + 1, HALF // 8):
            tile = jnp.where(group, 0.0, tiles[i])
            low = cols[i][0] * v[0] + cols[i][1] * v[1]
            high = cols[i][2] * v[2] + cols[i][3] * v[3]
            tiles[i] = tile - (low + high)
    return jnp.concatenate(result, axis=0)


def orthonormal_kernel(s_ref, basis_ref):
    sketch = s_ref[...].astype(F32)
    gram = fdot(sketch, sketch, 1, 1)
    first = lower_inverse(gram[:HALF, :HALF])
    across = fdot(gram[HALF:, :HALF], first, 1, 1)
    second = lower_inverse(gram[HALF:, HALF:] - fdot(across, across, 1, 1))
    top = fdot(first, sketch[:HALF], 1, 0)
    basis_ref[:HALF, :] = top.astype(BF16)
    rest = sketch[HALF:] - fdot(across, top, 1, 0)
    basis_ref[HALF:, :] = fdot(second, rest, 1, 0).astype(BF16)


def orthonormal(sketch):
    return pl.pallas_call(
        orthonormal_kernel,
        out_shape=jax.ShapeDtypeStruct(sketch.shape, BF16),
        in_specs=[VMEM],
        out_specs=VMEM,
        compiler_params=pltpu.CompilerParams(vmem_limit_bytes=40 << 20),
        cost_estimate=pl.CostEstimate(flops=2_000_000_000, bytes_accessed=2 << 20, transcendentals=0),
    )(sketch)


def stages_of(sk, lang):
    minor = 2 if sk % 2 == 0 else 1
    return (minor, sk // minor, lang)


def all_sum_kernel(sizes, term_ref, out_ref, acc, *scratch):
    depth = len(sizes)
    send = scratch[0]
    landing = scratch[1 : 1 + depth]
    gathered = scratch[1 + depth]
    send_sems, recv_sems, gsend_sems, grecv_sems = scratch[2 + depth :]
    s, j = lax.axis_index("sk"), lax.axis_index("lang")
    minor = sizes[0]
    mine = (lax.rem(s, minor), s // minor, j)

    def device(stage, index):
        if stage == 0:
            return (s - mine[0] + index, j)
        if stage == 1:
            return (index * minor + mine[0], j)
        return (s, index)

    def peers(stage):
        size = sizes[stage]
        return [(d, lax.rem(mine[stage] + d, size)) for d in range(1, size)]

    barrier = pltpu.get_barrier_semaphore()
    count = 0
    for stage in range(depth):
        for _, index in peers(stage):
            pl.semaphore_signal(
                barrier, inc=1, device_id=device(stage, index), device_id_type=pl.DeviceIdType.MESH
            )
            count += 1

    rows, width = term_ref.shape
    for b in range(width // LANE):
        acc[b * rows : (b + 1) * rows, :] = term_ref[:, b * LANE : (b + 1) * LANE].astype(F32)
    pl.semaphore_wait(barrier, count)

    base, size, slot = 0, acc.shape[0], 0
    spans = []
    for stage in range(depth):
        part = size // sizes[stage]
        copies = []
        for d, index in peers(stage):
            span = pl.ds(pl.multiple_of(base + index * part, part), part)
            send[span, :] = acc[span, :].astype(send.dtype)
            copy = pltpu.make_async_remote_copy(
                src_ref=send.at[span],
                dst_ref=landing[stage].at[d - 1],
                send_sem=send_sems.at[slot + d - 1],
                recv_sem=recv_sems.at[slot + d - 1],
                device_id=device(stage, index),
                device_id_type=pl.DeviceIdType.MESH,
            )
            copy.start()
            copies.append(copy)
        base = base + mine[stage] * part
        own = pl.ds(pl.multiple_of(base, part), part)
        for d, copy in enumerate(copies):
            copy.wait_recv()
        total = acc[own, :]
        for d in range(len(copies)):
            total = total + landing[stage][d].astype(F32)
        acc[own, :] = total
        for copy in copies:
            copy.wait_send()
        spans.append((base, part, slot))
        slot += len(copies)
        size = part

    own = pl.ds(pl.multiple_of(base, size), size)
    gathered[own, :] = acc[own, :].astype(gathered.dtype)
    for stage in reversed(range(depth)):
        base, part, slot = spans[stage]
        span = pl.ds(pl.multiple_of(base, part), part)
        copies = []
        for d, index in peers(stage):
            copy = pltpu.make_async_remote_copy(
                src_ref=gathered.at[span],
                dst_ref=gathered.at[span],
                send_sem=gsend_sems.at[slot + d - 1],
                recv_sem=grecv_sems.at[slot + d - 1],
                device_id=device(stage, index),
                device_id_type=pl.DeviceIdType.MESH,
            )
            copy.start()
            copies.append(copy)
        for copy in copies:
            copy.wait_recv()
        for copy in copies:
            copy.wait_send()
    for b in range(width // LANE):
        out_ref[:, b * LANE : (b + 1) * LANE] = gathered[b * rows : (b + 1) * rows, :]


def all_sum(term, wire, collective_id):
    sizes = stages_of(lax.axis_size("sk"), lax.axis_size("lang"))
    rows, width = term.shape
    flat = rows * width // LANE
    part, landing, slots = flat, [], 0
    for size in sizes:
        part //= size
        landing.append(pltpu.VMEM((max(1, size - 1), max(1, part), LANE), wire))
        slots += size - 1
    if part % 16 or part == 0:
        return lax.psum(term, ("sk", "lang"))
    return pl.pallas_call(
        functools.partial(all_sum_kernel, sizes),
        out_shape=jax.ShapeDtypeStruct((rows, width), wire),
        in_specs=[VMEM],
        out_specs=VMEM,
        scratch_shapes=[
            pltpu.VMEM((flat, LANE), F32),
            pltpu.VMEM((flat, LANE), wire),
            *landing,
            pltpu.VMEM((flat, LANE), wire),
        ]
        + [pltpu.SemaphoreType.DMA((slots,))] * 4,
        compiler_params=pltpu.CompilerParams(
            collective_id=collective_id, has_side_effects=True, vmem_limit_bytes=40 << 20
        ),
    )(term)


def regroup_kernel(lang_count, per_owner, emb_ref, basis_ref, langs_ref, out_ref, target, send, send_sems, recv_sems):
    s, j = lax.axis_index("sk"), lax.axis_index("lang")
    barrier = pltpu.get_barrier_semaphore()
    others = [lax.rem(j + d, lang_count) for d in range(1, lang_count)]
    for index in others:
        pl.semaphore_signal(barrier, inc=1, device_id=(s, index), device_id_type=pl.DeviceIdType.MESH)
    rows = emb_ref.shape[0]
    block = per_owner * CAP
    langs = langs_ref[...]
    padded = -(-LANGS // 16) * 16
    member = lax.broadcasted_iota(jnp.int32, (padded, rows), 0) == langs
    upto = lax.broadcasted_iota(jnp.int32, (rows, rows), 0) <= lax.broadcasted_iota(jnp.int32, (rows, rows), 1)
    earlier = bdot(member.astype(F32).astype(BF16), upto.astype(F32).astype(BF16), 1, 0)
    position = jnp.sum(jnp.where(member, earlier, 0.0), axis=0, keepdims=True).astype(jnp.int32) - 1
    target[...] = lax.rem(langs, lang_count) * block + lax.div(langs, lang_count) * CAP + position
    coords = bdot(emb_ref[...], basis_ref[...], 1, 1).astype(BF16)

    def part(index):
        slots = lax.broadcasted_iota(jnp.int32, (block, rows), 0) + index * block
        chosen = (slots == target[...]).astype(F32).astype(BF16)
        return bdot(chosen, coords, 1, 0).astype(BF16)

    pl.semaphore_wait(barrier, lang_count - 1)
    here = pl.ds(pl.multiple_of(j * block, block), block)
    copies = []
    for d, index in enumerate(others):
        there = pl.ds(d * block, block)
        send[there, :] = part(index)
        copy = pltpu.make_async_remote_copy(
            src_ref=send.at[there],
            dst_ref=out_ref.at[here],
            send_sem=send_sems.at[d],
            recv_sem=recv_sems.at[d],
            device_id=(s, index),
            device_id_type=pl.DeviceIdType.MESH,
        )
        copy.start()
        copies.append(copy)
    out_ref[here, :] = part(j)
    for copy in copies:
        copy.wait()


def regroup(embeddings, basis, lang_ids):
    lang_count = lax.axis_size("lang")
    per_owner = (LANGS + lang_count - 1) // lang_count
    rows = embeddings.shape[0]
    total = lang_count * per_owner * CAP
    return pl.pallas_call(
        functools.partial(regroup_kernel, lang_count, per_owner),
        out_shape=jax.ShapeDtypeStruct((total, SKETCH), BF16),
        in_specs=[VMEM] * 3,
        out_specs=VMEM,
        scratch_shapes=[
            pltpu.VMEM((1, rows), jnp.int32),
            pltpu.VMEM((total, SKETCH), BF16),
            pltpu.SemaphoreType.DMA((lang_count - 1,)),
            pltpu.SemaphoreType.DMA((lang_count - 1,)),
        ],
        compiler_params=pltpu.CompilerParams(
            collective_id=2, has_side_effects=True, vmem_limit_bytes=40 << 20
        ),
    )(embeddings, basis, lang_ids.reshape(1, rows))


WIRE = (F32, F32)


def on_device(embeddings, omega, lang_ids):
    first_term = bdot(omega, embeddings, 0, 0)
    first_basis = orthonormal(all_sum(first_term, WIRE[0], 0))
    scores = bdot(embeddings, first_basis, 1, 1).astype(BF16)
    second_term = bdot(scores, embeddings, 0, 0)
    second_basis = orthonormal(all_sum(second_term, WIRE[1], 1))
    return regroup(embeddings, second_basis, lang_ids)


def solution(mesh):
    spec = P(("sk", "lang"), None)
    return jax.shard_map(
        on_device, mesh=mesh, in_specs=(spec, spec, spec), out_specs=spec, check_vma=False
    )
```

profile of v0, /device:TPU:0, one launch (start us, length us, event | category | flops | bytes accessed | tf_op | source)
XLA Modules:
  0.0 114.3 jit_solution(6032310092722590355)
XLA Ops:
  0.0 0.0 copy-start
  0.0 1.0 copy-done
  1.0 2.3 %fusion.1.term_ref = f32[256,1024]{1,0:T(8,128)S(1)} fusion(bf16[1024,256]{1,0:T(8,128)(2,1)S(1)} %copy-done, bf16[1024,1024]{1,0:T(8,128)(2,1)} %emb_ref.1), kind=kOutput, calls=%fused_computation.2 | convolution fusion | flops 536870912 | bytes 3670016 | tf_op jit(solution)/shard_map/dot_general | solution.py:28
  3.4 31.8 %shard_map.37.s_ref = f32[256,1024]{1,0:T(8,128)S(1)} custom-call(f32[256,1024]{1,0:T(8,128)S(1)} %fusion.1.term_ref), custom_call_target="tpu_custom_call" | custom-call | tf_op jit(solution)/shard_map/pallas_call | solution.py:209
  35.2 0.0 copy-start.1
  35.2 13.6 %shard_map.38 = bf16[256,1024]{1,0:T(8,128)(2,1)S(1)} custom-call(f32[256,1024]{1,0:T(8,128)S(1)} %shard_map.37.s_ref), custom_call_target="tpu_custom_call" | custom-call | flops 2000000000 | bytes 2097152 | tf_op jit(solution)/shard_map/pallas_call | solution.py:91
  48.8 0.0 copy-done.1
  48.8 2.3 %fusion.term_ref = f32[256,1024]{1,0:T(8,128)} fusion(bf16[1024,1024]{1,0:T(8,128)(2,1)S(1)} %copy-done.1, bf16[256,1024]{1,0:T(8,128)(2,1)S(1)} %shard_map.38), kind=kOutput, calls=%fused_computation.1 | convolution fusion | flops 1074003968 | bytes 3670016 | tf_op jit(solution)/shard_map/dot_general | solution.py:28
  51.1 0.0 copy-start.2
  51.1 1.2 %copy-done.2 = f32[256,1024]{1,0:T(8,128)S(1)} copy-done((f32[256,1024]{1,0:T(8,128)S(1)}, f32[256,1024]{1,0:T(8,128)}, u32[]{:S(2)}) %copy-start.2) | copy-done | bytes 1048600
  52.3 28.6 %shard_map.39.s_ref = f32[256,1024]{1,0:T(8,128)S(1)} custom-call(f32[256,1024]{1,0:T(8,128)S(1)} %copy-done.2), custom_call_target="tpu_custom_call" | custom-call | tf_op jit(solution)/shard_map/pallas_call | solution.py:209
  80.9 0.0 copy-start.3
  80.9 13.8 %shard_map.40.basis_ref = bf16[256,1024]{1,0:T(8,128)(2,1)S(1)} custom-call(f32[256,1024]{1,0:T(8,128)S(1)} %shard_map.39.s_ref), custom_call_target="tpu_custom_call" | custom-call | flops 2000000000 | bytes 2097152 | tf_op jit(solution)/shard_map/pallas_call | solution.py:91
  94.7 0.0 copy-done.3
  94.7 18.8 %shard_map.41 = bf16[1536,256]{1,0:T(8,128)(2,1)S(1)} custom-call(bf16[1024,1024]{1,0:T(8,128)(2,1)S(1)} %copy-done.1, bf16[256,1024]{1,0:T(8,128)(2,1)S(1)} %shard_map.40.basis_ref, s32[1,1024]{1,0:T(1,128)S(1)} %bitcast.6), custom_call_target="tpu_custom_call" | custom-call | tf_op jit(solution)/shard_map/pallas_call | solution.py:275
  113.5 0.9 copy.5
Async XLA Ops:
  0.0 1.0 copy-start
  35.2 13.6 %copy-start.1 = (bf16[1024,1024]{1,0:T(8,128)(2,1)S(1)}, bf16[1024,1024]{1,0:T(8,128)(2,1)}, u32[]{:S(2)}) copy-start(bf16[1024,1024]{1,0:T(8,128)(2,1)} %emb_ref.1) | copy-start | bytes 6291460
  51.1 1.2 %copy-start.2 = (f32[256,1024]{1,0:T(8,128)S(1)}, f32[256,1024]{1,0:T(8,128)}, u32[]{:S(2)}) copy-start(f32[256,1024]{1,0:T(8,128)} %fusion.term_ref) | copy-start | bytes 3145732
  80.9 13.8 %copy-start.3 = (s32[1024,1]{0,1:T(1,128)S(1)}, s32[1024,1]{0,1:T(1,128)}, u32[]{:S(2)}) copy-start(s32[1024,1]{0,1:T(1,128)} %param.5) | copy-start | bytes 12292
where the time goes:
time: 116 us; the launch traced here: 114 us
  Pallas kernels  107 us (92%)
  matrix products  4.57 us (4%)
  local copies, waits for them, and re-layouts  3.16 us (3%)
    pallas_call x2, Pallas kernels, all_sum(): pl.pallas_call(functools.partial(all_sum_kernel, sizes), out_shape=jax.Sh...  60.4 us
    pallas_call x2, Pallas kernels, orthonormal(): pl.pallas_call(orthonormal_kernel, out_shape=jax.ShapeDtypeStruct(sketch....  27.4 us
    pallas_call x1, Pallas kernels, regroup(): pl.pallas_call(functools.partial(regroup_kernel, lang_count, per_owner),...  18.8 us
    dot_general x2, matrix products, bdot(): lax.dot_general(a, b, (((ca,), (cb,)), ((), ())), preferred_element_type=...  4.57 us
    unnamed x9, local copies, waits for them, and re-layouts  3.16 us

commit v1 on v0

--- a/solution.py
+++ b/solution.py
@@ -28,13 +28,15 @@
     return lax.dot_general(a, b, (((ca,), (cb,)), ((), ())), preferred_element_type=F32)
 
 
-def lower_inverse(a):
+def lower_inverse(a, hooks=None):
     lane = lax.broadcasted_iota(jnp.int32, (1, LANE), 1)
     sub = lax.broadcasted_iota(jnp.int32, (8, LANE), 0)
     lane8 = lax.broadcasted_iota(jnp.int32, (8, LANE), 1)
     tiles = [a[8 * i : 8 * i + 8, :] for i in range(HALF // 8)]
     result = []
     for k in range(0, HALF, 4):
+        if hooks and k in hooks:
+            hooks[k]()
         t, s = k // 8, k % 8
         cols = {
             i: [jnp.broadcast_to(tiles[i][:, k + j : k + j + 1], (8, LANE)) for j in range(4)]
@@ -289,10 +291,275 @@
     )(embeddings, basis, lang_ids.reshape(1, rows))
 
 
+class Piece:
+    def __init__(self, sizes, mine, device, acc, landing, gathered, sems):
+        self.sizes, self.mine, self.device = sizes, mine, device
+        self.acc, self.landing, self.gathered, self.sems = acc, landing, gathered, sems
+        self.base, self.size, self.slot = 0, acc.shape[0], 0
+        self.spans, self.copies = [], []
+
+    def copy(self, src, dst, slot, stage, index):
+        copy = pltpu.make_async_remote_copy(
+            src_ref=src,
+            dst_ref=dst,
+            send_sem=self.sems.at[0, slot],
+            recv_sem=self.sems.at[1, slot],
+            device_id=self.device(stage, index),
+            device_id_type=pl.DeviceIdType.MESH,
+        )
+        copy.start()
+        self.copies.append(copy)
+
+    def send(self, stage):
+        size = self.sizes[stage]
+        part = self.size // size
+        for d in range(1, size):
+            index = lax.rem(self.mine[stage] + d, size)
+            span = pl.ds(pl.multiple_of(self.base + index * part, part), part)
+            self.copy(self.acc.at[span], self.landing[stage].at[d - 1], self.slot + d - 1, stage, index)
+
+    def add(self, stage):
+        size = self.sizes[stage]
+        part = self.size // size
+        base = self.base + self.mine[stage] * part
+        own = pl.ds(pl.multiple_of(base, part), part)
+        for copy in self.copies:
+            copy.wait_recv()
+        total = self.acc[own, :]
+        for d in range(1, size):
+            total = total + self.landing[stage][d - 1]
+        last = stage == len(self.sizes) - 1
+        (self.gathered if last else self.acc)[own, :] = total
+        for copy in self.copies:
+            copy.wait_send()
+        self.copies = []
+        self.base, self.size, self.slot = base, part, self.slot + size - 1
+        self.spans.append((base, part))
+
+    def spread(self, stage):
+        base, part = self.spans[stage]
+        span = pl.ds(pl.multiple_of(base, part), part)
+        for d in range(1, self.sizes[stage]):
+            index = lax.rem(self.mine[stage] + d, self.sizes[stage])
+            self.copy(self.gathered.at[span], self.gathered.at[span], self.slot + d - 1, stage, index)
+        self.slot += self.sizes[stage] - 1
+
+    def land(self):
+        for copy in self.copies:
+            copy.wait_recv()
+        for copy in self.copies:
+            copy.wait_send()
+        self.copies = []
+
+    def put(self, term):
+        for b in range(term.shape[1] // LANE):
+            self.acc[b * HALF : (b + 1) * HALF, :] = term[:, b * LANE : (b + 1) * LANE]
+
+    def get(self):
+        blocks = self.gathered.shape[0] // HALF
+        return jnp.concatenate([self.gathered[b * HALF : (b + 1) * HALF, :] for b in range(blocks)], axis=1)
+
+
+def whole_kernel(sizes, per_owner, emb_ref, omega_ref, langs_ref, out_ref, *scratch):
+    minor, lang_count = sizes[0], sizes[2]
+    s, j = lax.axis_index("sk"), lax.axis_index("lang")
+    mine = (lax.rem(s, minor), s // minor, j)
+    chosen, outgoing, out_sems = scratch[:3]
+
+    def device(stage, index):
+        if stage == 0:
+            return (s - mine[0] + index, j)
+        if stage == 1:
+            return (index * minor + mine[0], j)
+        return (s, index)
+
+    pieces = []
+    for n in range(4):
+        part = scratch[3 + 6 * n : 9 + 6 * n]
+        pieces.append(Piece(sizes, mine, device, part[0], part[1:4], part[4], part[5]))
+    a1, b1, a2, b2 = pieces
+
+    barrier = pltpu.get_barrier_semaphore()
+    count = 0
+    for stage in range(3):
+        for d in range(1, sizes[stage]):
+            pl.semaphore_signal(
+                barrier,
+                inc=1,
+                device_id=device(stage, lax.rem(mine[stage] + d, sizes[stage])),
+                device_id_type=pl.DeviceIdType.MESH,
+            )
+            count += 1
+
+    block = per_owner * CAP
+    rows = emb_ref.shape[0]
+    others = [lax.rem(j + d, lang_count) for d in range(1, lang_count)]
+
+    def choose():
+        langs = langs_ref[...]
+        padded = -(-LANGS // 16) * 16
+        member = lax.broadcasted_iota(jnp.int32, (padded, rows), 0) == langs
+        upto = lax.broadcasted_iota(jnp.int32, (rows, rows), 0) <= lax.broadcasted_iota(jnp.int32, (rows, rows), 1)
+        earlier = bdot(member.astype(F32).astype(BF16), upto.astype(F32).astype(BF16), 1, 0)
+        position = jnp.sum(jnp.where(member, earlier, 0.0), axis=0, keepdims=True).astype(jnp.int32) - 1
+        target = lax.rem(langs, lang_count) * block + lax.div(langs, lang_count) * CAP + position
+        slots = lax.broadcasted_iota(jnp.int32, (block, rows), 0)
+        for n, index in enumerate(others + [j]):
+            chosen[n * block : (n + 1) * block, :] = (slots + index * block == target).astype(F32).astype(BF16)
+
+    def power(piece, basis):
+        scores = bdot(basis, emb_ref[...], 1, 1).astype(BF16)
+        piece.put(bdot(scores, emb_ref[...], 1, 0))
+
+    def hand_out(basis, half):
+        coords = bdot(emb_ref[...], basis, 1, 1).astype(BF16)
+        here = pl.ds(pl.multiple_of(j * block, block), block)
+        lanes = pl.ds(half * HALF, HALF)
+        copies = []
+        for n, index in enumerate(others):
+            span = pl.ds(n * block, block)
+            outgoing[half, span, :] = bdot(chosen[span, :], coords, 1, 0).astype(BF16)
+            copy = pltpu.make_async_remote_copy(
+                src_ref=outgoing.at[half, span],
+                dst_ref=out_ref.at[here, lanes],
+                send_sem=out_sems.at[0, half, n],
+                recv_sem=out_sems.at[1, half, n],
+                device_id=(s, index),
+                device_id_type=pl.DeviceIdType.MESH,
+            )
+            copy.start()
+            copies.append(copy)
+        own = chosen[len(others) * block : (len(others) + 1) * block, :]
+        out_ref[here, half * HALF : (half + 1) * HALF] = bdot(own, coords, 1, 0).astype(BF16)
+        return copies
+
+    a1.put(bdot(omega_ref[:, :HALF], emb_ref[...], 0, 0))
+    pl.semaphore_wait(barrier, count)
+    a1.send(0)
+    b1.put(bdot(omega_ref[:, HALF:], emb_ref[...], 0, 0))
+    b1.send(0)
+    a1.add(0)
+    a1.send(1)
+    b1.add(0)
+    b1.send(1)
+    choose()
+    a1.add(1)
+    a1.send(2)
+    b1.add(1)
+    b1.send(2)
+    a1.add(2)
+    a1.spread(2)
+    b1.add(2)
+    b1.spread(2)
+    a1.land()
+    a1.spread(1)
+    b1.land()
+    a1.land()
+    a1.spread(0)
+    b1.spread(1)
+    a1.land()
+
+    def b1_last():
+        b1.land()
+        b1.spread(0)
+
+    first = a1.get()
+    inverse = lower_inverse(fdot(first, first, 1, 1), {96: b1_last})
+    top = fdot(inverse, first, 1, 0)
+    power(a2, top.astype(BF16))
+    a2.send(0)
+    b1.land()
+
+    second = b1.get()
+    across = fdot(fdot(second, first, 1, 1), inverse, 1, 1)
+    corner = fdot(second, second, 1, 1) - fdot(across, across, 1, 1)
+    a2.add(0)
+    a2.send(1)
+    rest = second - fdot(across, top, 1, 0)
+    inverse = lower_inverse(corner)
+    a2.add(1)
+    a2.send(2)
+    power(b2, fdot(inverse, rest, 1, 0).astype(BF16))
+    b2.send(0)
+    a2.add(2)
+    a2.spread(2)
+    b2.add(0)
+    b2.send(1)
+    a2.land()
+    a2.spread(1)
+    b2.add(1)
+    b2.send(2)
+    a2.land()
+    a2.spread(0)
+    b2.add(2)
+    b2.spread(2)
+    a2.land()
+
+    def b2_middle():
+        b2.land()
+        b2.spread(1)
+
+    def b2_last():
+        b2.land()
+        b2.spread(0)
+
+    first = a2.get()
+    inverse = lower_inverse(fdot(first, first, 1, 1), {32: b2_middle, 120: b2_last})
+    top = fdot(inverse, first, 1, 0)
+    copies = hand_out(top.astype(BF16), 0)
+    b2.land()
+    second = b2.get()
+    across = fdot(fdot(second, first, 1, 1), inverse, 1, 1)
+    corner = fdot(second, second, 1, 1) - fdot(across, across, 1, 1)
+    rest = second - fdot(across, top, 1, 0)
+    inverse = lower_inverse(corner)
+    copies += hand_out(fdot(inverse, rest, 1, 0).astype(BF16), 1)
+    for copy in copies:
+        copy.wait()
+
+
+def in_one_kernel(sizes, embeddings, omega, lang_ids):
+    rows, width = embeddings.shape
+    lang_count = sizes[2]
+    per_owner = (LANGS + lang_count - 1) // lang_count
+    total = lang_count * per_owner * CAP
+    flat = HALF * width // LANE
+    slots = 2 * sum(size - 1 for size in sizes)
+    part, landing = flat, []
+    for size in sizes:
+        part //= size
+        landing.append(pltpu.VMEM((max(1, size - 1), part, LANE), F32))
+    piece = [
+        pltpu.VMEM((flat, LANE), F32),
+        *landing,
+        pltpu.VMEM((flat, LANE), F32),
+        pltpu.SemaphoreType.DMA((2, slots)),
+    ]
+    return pl.pallas_call(
+        functools.partial(whole_kernel, sizes, per_owner),
+        out_shape=jax.ShapeDtypeStruct((total, SKETCH), BF16),
+        in_specs=[VMEM] * 3,
+        out_specs=VMEM,
+        scratch_shapes=[
+            pltpu.VMEM((total, rows), BF16),
+            pltpu.VMEM((2, (lang_count - 1) * per_owner * CAP, HALF), BF16),
+            pltpu.SemaphoreType.DMA((2, 2, lang_count - 1)),
+            *(piece * 4),
+        ],
+        compiler_params=pltpu.CompilerParams(
+            collective_id=3, has_side_effects=True, vmem_limit_bytes=48 << 20
+        ),
+    )(embeddings, omega, lang_ids.reshape(1, rows))
+
+
 WIRE = (F32, F32)
 
 
 def on_device(embeddings, omega, lang_ids):
+    sizes = stages_of(lax.axis_size("sk"), lax.axis_size("lang"))
+    flat = HALF * embeddings.shape[1] // LANE
+    if flat % (8 * sizes[0] * sizes[1] * sizes[2]) == 0:
+        return in_one_kernel(sizes, embeddings, omega, lang_ids)
     first_term = bdot(omega, embeddings, 0, 0)
     first_basis = orthonormal(all_sum(first_term, WIRE[0], 0))
     scores = bdot(embeddings, first_basis, 1, 1).astype(BF16)

time: 116 us -> 98.6 us (0.85); the launches traced: 114 us -> 98.4 us
  Pallas kernels: 107 us -> 94.2 us
  matrix products: 4.57 us -> 0 us
    pallas_call x5 -> x1, Pallas kernels: 107 us -> 94.2 us  [in_one_kernel(): pl.pallas_call(functools.partial(whole_kernel, sizes, per_owner), out_sha...]
    dot_general x2 -> x0, matrix products: 4.57 us -> none  [bdot(): lax.dot_general(a, b, (((ca,), (cb,)), ((), ())), preferred_element_type=...]
    unnamed x9 -> x7, local copies, waits for them, and re-layouts: 3.16 us -> 4.2 us
where the time goes in v1:
time: 98.6 us; the launch traced here: 98.4 us
  Pallas kernels  94.2 us (96%)
  local copies, waits for them, and re-layouts  4.2 us (4%)
    pallas_call x1, Pallas kernels, in_one_kernel(): pl.pallas_call(functools.partial(whole_kernel, sizes, per_owner), out_sha...  94.2 us
    unnamed x7, local copies, waits for them, and re-layouts  4.2 us

profile of v1, /device:TPU:0, one launch (start us, length us, event | category | flops | bytes accessed | tf_op | source)
XLA Modules:
  0.0 98.4 jit_solution(12121338629882218598)
XLA Ops:
  0.0 0.0 copy-start
  0.0 1.6 %copy-done = bf16[1024,1024]{1,0:T(8,128)(2,1)S(1)} copy-done((bf16[1024,1024]{1,0:T(8,128)(2,1)S(1)}, bf16[1024,1024]{1,0:T(8,128)(2,1)}, u32[]{:S(2)}) %copy-start) | copy-done | bytes 2097176
  1.6 0.0 copy-start.1
  1.6 1.0 %copy-done.1 = bf16[1024,256]{1,0:T(8,128)(2,1)S(1)} copy-done((bf16[1024,256]{1,0:T(8,128)(2,1)S(1)}, bf16[1024,256]{1,0:T(8,128)(2,1)}, u32[]{:S(2)}) %copy-start.1) | copy-done | bytes 524312
  2.6 0.0 copy-start.2
  2.6 0.7 copy-done.2
  3.3 94.2 %shard_map.37 = bf16[1536,256]{1,0:T(8,128)(2,1)S(1)} custom-call(bf16[1024,1024]{1,0:T(8,128)(2,1)S(1)} %copy-done, bf16[1024,256]{1,0:T(8,128)(2,1)S(1)} %copy-done.1, s32[1,1024]{1,0:T(1,128)S(1)} %bitcast.1), custom_call_target="tpu_custom_call" | custom-call | tf_op jit(solution)/shard_map/pallas_call | solution.py:538
  97.5 0.9 copy.5
Async XLA Ops:
  0.0 1.6 %copy-start = (bf16[1024,1024]{1,0:T(8,128)(2,1)S(1)}, bf16[1024,1024]{1,0:T(8,128)(2,1)}, u32[]{:S(2)}) copy-start(bf16[1024,1024]{1,0:T(8,128)(2,1)} %emb_ref.1) | copy-start | bytes 6291460
  1.6 1.0 %copy-start.1 = (bf16[1024,256]{1,0:T(8,128)(2,1)S(1)}, bf16[1024,256]{1,0:T(8,128)(2,1)}, u32[]{:S(2)}) copy-start(bf16[1024,256]{1,0:T(8,128)(2,1)} %omega_ref.1) | copy-start | bytes 1572868
  2.6 0.7 copy-start.2

commit v2 on v1

--- a/solution.py
+++ b/solution.py
@@ -360,7 +360,7 @@
         return jnp.concatenate([self.gathered[b * HALF : (b + 1) * HALF, :] for b in range(blocks)], axis=1)
 
 
-def whole_kernel(sizes, per_owner, emb_ref, omega_ref, langs_ref, out_ref, *scratch):
+def whole_kernel(sizes, per_owner, emb_ref, term_ref, langs_ref, out_ref, *scratch):
     minor, lang_count = sizes[0], sizes[2]
     s, j = lax.axis_index("sk"), lax.axis_index("lang")
     mine = (lax.rem(s, minor), s // minor, j)
@@ -433,10 +433,10 @@
         out_ref[here, half * HALF : (half + 1) * HALF] = bdot(own, coords, 1, 0).astype(BF16)
         return copies
 
-    a1.put(bdot(omega_ref[:, :HALF], emb_ref[...], 0, 0))
+    a1.put(term_ref[:HALF, :])
     pl.semaphore_wait(barrier, count)
     a1.send(0)
-    b1.put(bdot(omega_ref[:, HALF:], emb_ref[...], 0, 0))
+    b1.put(term_ref[HALF:, :])
     b1.send(0)
     a1.add(0)
     a1.send(1)
@@ -518,7 +518,7 @@
         copy.wait()
 
 
-def in_one_kernel(sizes, embeddings, omega, lang_ids):
+def in_one_kernel(sizes, embeddings, term, lang_ids):
     rows, width = embeddings.shape
     lang_count = sizes[2]
     per_owner = (LANGS + lang_count - 1) // lang_count
@@ -549,18 +549,18 @@
         compiler_params=pltpu.CompilerParams(
             collective_id=3, has_side_effects=True, vmem_limit_bytes=48 << 20
         ),
-    )(embeddings, omega, lang_ids.reshape(1, rows))
+    )(embeddings, term, lang_ids.reshape(1, rows))
 
 
 WIRE = (F32, F32)
 
 
 def on_device(embeddings, omega, lang_ids):
+    first_term = bdot(omega, embeddings, 0, 0)
     sizes = stages_of(lax.axis_size("sk"), lax.axis_size("lang"))
     flat = HALF * embeddings.shape[1] // LANE
     if flat % (8 * sizes[0] * sizes[1] * sizes[2]) == 0:
-        return in_one_kernel(sizes, embeddings, omega, lang_ids)
-    first_term = bdot(omega, embeddings, 0, 0)
+        return in_one_kernel(sizes, embeddings, first_term, lang_ids)
     first_basis = orthonormal(all_sum(first_term, WIRE[0], 0))
     scores = bdot(embeddings, first_basis, 1, 1).astype(BF16)
     second_term = bdot(scores, embeddings, 0, 0)

time: 98.6 us -> 98.7 us (level)
  matrix products: 0 us -> 2.31 us
  local copies, waits for them, and re-layouts: 4.2 us -> 1.93 us
    dot_general x0 -> x1, matrix products: none -> 2.31 us  [bdot(): lax.dot_general(a, b, (((ca,), (cb,)), ((), ())), preferred_element_type=...]
    unnamed x7, local copies, waits for them, and re-layouts: 4.2 us -> 1.93 us
where the time goes in v2:
time: 98.7 us; the launch traced here: 98.6 us
  Pallas kernels  94.3 us (96%)
  matrix products  2.31 us (2%)
  local copies, waits for them, and re-layouts  1.93 us (2%)
    pallas_call x1, Pallas kernels, in_one_kernel(): pl.pallas_call(functools.partial(whole_kernel, sizes, per_owner), out_sha...  94.3 us
    dot_general x1, matrix products, bdot(): lax.dot_general(a, b, (((ca,), (cb,)), ((), ())), preferred_element_type=...  2.31 us

profile of v2, /device:TPU:0, one launch (start us, length us, event | category | flops | bytes accessed | tf_op | source)
XLA Modules:
  0.0 98.6 jit_solution(10094084519952945536)
XLA Ops:
  0.0 0.0 copy-start
  0.0 0.0 copy-start.1
  0.0 0.0 copy-start.2
  0.0 1.0 %copy-done = bf16[1024,256]{1,0:T(8,128)(2,1)S(1)} copy-done((bf16[1024,256]{1,0:T(8,128)(2,1)S(1)}, bf16[1024,256]{1,0:T(8,128)(2,1)}, u32[]{:S(2)}) %copy-start) | copy-done | bytes 524312
  1.0 2.3 %fusion.term_ref = f32[256,1024]{1,0:T(8,128)S(1)} fusion(bf16[1024,256]{1,0:T(8,128)(2,1)S(1)} %copy-done, bf16[1024,1024]{1,0:T(8,128)(2,1)} %emb_ref.1), kind=kOutput, calls=%fused_computation | convolution fusion | flops 536870912 | bytes 3670016 | tf_op jit(solution)/shard_map/dot_general | solution.py:28
  3.4 0.0 copy-done.1
  3.4 0.0 copy-done.2
  3.4 94.3 %shard_map.37 = bf16[1536,256]{1,0:T(8,128)(2,1)S(1)} custom-call(bf16[1024,1024]{1,0:T(8,128)(2,1)S(1)} %copy-done.1, f32[256,1024]{1,0:T(8,128)S(1)} %fusion.term_ref, s32[1,1024]{1,0:T(1,128)S(1)} %bitcast.3), custom_call_target="tpu_custom_call" | custom-call | tf_op jit(solution)/shard_map/pallas_call | solution.py:538
  97.7 0.9 copy.5
Async XLA Ops:
  0.0 1.0 %copy-start = (bf16[1024,256]{1,0:T(8,128)(2,1)S(1)}, bf16[1024,256]{1,0:T(8,128)(2,1)}, u32[]{:S(2)}) copy-start(bf16[1024,256]{1,0:T(8,128)(2,1)} %param.4) | copy-start | bytes 1572868
  0.0 3.4 %copy-start.1 = (bf16[1024,1024]{1,0:T(8,128)(2,1)S(1)}, bf16[1024,1024]{1,0:T(8,128)(2,1)}, u32[]{:S(2)}) copy-start(bf16[1024,1024]{1,0:T(8,128)(2,1)} %emb_ref.1) | copy-start | bytes 6291460
  0.0 3.4 %copy-start.2 = (s32[1024,1]{0,1:T(1,128)S(1)}, s32[1024,1]{0,1:T(1,128)}, u32[]{:S(2)}) copy-start(s32[1024,1]{0,1:T(1,128)} %param.5) | copy-start | bytes 12292
